TPU v7x, 32 devices: a whole 2x2x4 slice. The times are simulated.
32 devices in a mesh: section: 2 (over y), dp: 16 (over z, x, core).
Axes of the slice: x: 2, y: 2, z: 4, core: 2. Of those that a mesh axis runs over, the one named last changes fastest.
Arguments:
- tokens_in: bfloat16 [2, 1024, 768], P(None, 'dp'), may hold values from -6 to 6
- segment_ids: int32 [2, 1024], P(None, 'dp'), may hold values from 0 to 6, as said below
- out_grad: bfloat16 [2, 1024, 768], P(None, 'dp'), may hold values from -6 to 6
- qkv_weight: bfloat16 [2, 768, 2304], P('section', 'dp'), may hold values from -0.21875 to 0.21875
- attn_out_weight: bfloat16 [2, 768, 768], P('section', 'dp'), may hold values from -1.75 to 1.75
- mlp_in_weight: bfloat16 [2, 768, 2304], P('section', 'dp'), may hold values from -0.21875 to 0.21875
- mlp_out_weight: bfloat16 [2, 1152, 768], P('section', 'dp'), may hold values from -0.1875 to 0.1875
- attn_gain: bfloat16 [2, 768], P('section', 'dp'), may hold values from 0.25 to 1.75
- mlp_gain: bfloat16 [2, 768], P('section', 'dp'), may hold values from 0.25 to 1.75
Outputs:
- layer_outputs: bfloat16 [2, 2, 1024, 768], P('section', None, 'dp')
- input_grads: bfloat16 [2, 2, 1024, 768], P('section', None, 'dp')
- qkv_grad: float32 [2, 768, 2304], P('section', 'dp')
- attn_out_grad: float32 [2, 768, 768], P('section', 'dp')
- mlp_in_grad: float32 [2, 768, 2304], P('section', 'dp')
- mlp_out_grad: float32 [2, 1152, 768], P('section', 'dp')
- attn_gain_grad: float32 [2, 768], P('section', 'dp')
- mlp_gain_grad: float32 [2, 768], P('section', 'dp')
Inputs may be any that keep to these rules, and one draw needn't show every extreme that they name: `segment_ids`: within each sequence of 1024 tokens the numbers start at 0, never fall and rise by exactly one at each document start: 3 starts lie among positions 1 to 62 and 3 among positions 962 to 1023 of the sequence, none elsewhere.
All inputs are finite; a program needn't handle non-finite values.
Results may differ from a plain program's by a relative error of at most 0.024.
Values may be sent and summed in bfloat16 or wider, within the bound.
No kernel may reach another device: no remote copies, remote signals or barrier semaphores. Data moves between devices by JAX's collectives and lax.ppermute only.
A program may use at most 192 MiB of HBM per device.

v0:
```python
import math

import jax
import jax.numpy as jnp
from jax import lax
from jax.sharding import PartitionSpec as P

HEAD_DIM = 64
GROUP = 16
HALF_WIN = 64


local_log_base = math.log(10000.0)
global_log_base = math.log(160000.0)
masked_score = -1e30


def from_partner(x, axis, apart):
    return lax.ppermute(x, axis, [(i, i ^ 1 << apart) for i in range(lax.axis_size(axis))])


def passed_along(value, axis, steps):
    count = lax.axis_size(axis)
    initial, last = (max(0, -steps), min(count, count - steps))
    return lax.ppermute(value, axis, [(source, source + steps) for source in range(initial, last)])


def normalize(values, gain_row):
    center = values - jnp.mean(values, -1, keepdims=True)
    spread = jnp.mean(center * center, -1, keepdims=True)
    return center * lax.rsqrt(spread + 1e-05) * gain_row


def angles(positions, log_base, head_dim):
    half_dim = head_dim // 2
    fraction = (2 * jnp.arange(half_dim)).astype(jnp.float32) / head_dim
    inverse = jnp.exp(-fraction * log_base)
    angle_table = positions.astype(jnp.float32)[:, None] * inverse[None, :]
    angle_table = jnp.concatenate([angle_table, angle_table], -1)
    return (jnp.cos(angle_table)[:, None, :], jnp.sin(angle_table)[:, None, :])


def rotate(values, cosine, sine_table):
    half_dim = values.shape[-1] // 2
    turned = jnp.concatenate([-values[..., half_dim:], values[..., :half_dim]], -1)
    return values * cosine + turned * sine_table


def unrotate(grad_rows, cosine, sine_table):
    half_dim = grad_rows.shape[-1] // 2
    scaled = grad_rows * sine_table
    turned = jnp.concatenate([scaled[..., half_dim:], -scaled[..., :half_dim]], -1)
    return grad_rows * cosine + turned


def activate(gate_up):
    half_width = gate_up.shape[-1] // 2
    return jax.nn.gelu(gate_up[:, :half_width], approximate=False) * gate_up[:, half_width:]


def upper_flag(group_pos, bit_index):
    return group_pos // (1 << bit_index) % 2 == 1


def spread_segments(local_ids, group_pos):
    gathered = local_ids
    for bit_index in range(GROUP.bit_length() - 1):
        partner = from_partner(gathered, "dp", bit_index)
        gathered = jnp.where(
            upper_flag(group_pos, bit_index),
            jnp.concatenate([partner, gathered], 1),
            jnp.concatenate([gathered, partner], 1),
        )
    return gathered


def spread_keys(local_keys, group_pos):
    gathered = local_keys
    for bit_index in range(GROUP.bit_length() - 1):
        partner = from_partner(gathered, "dp", bit_index)
        gathered = jnp.where(
            upper_flag(group_pos, bit_index),
            jnp.concatenate([partner, gathered], 0),
            jnp.concatenate([gathered, partner], 0),
        )
    return gathered


def spread_queries(query_rows, query_stats, group_pos):
    rows_all = query_rows
    stats_all = query_stats
    for bit_index in range(GROUP.bit_length() - 1):
        partner_rows = from_partner(rows_all, "dp", bit_index)
        partner_stats = from_partner(stats_all, "dp", bit_index)
        is_upper = upper_flag(group_pos, bit_index)
        rows_all = jnp.where(
            is_upper,
            jnp.concatenate([partner_rows, rows_all], 0),
            jnp.concatenate([rows_all, partner_rows], 0),
        )
        stats_all = jnp.where(
            is_upper,
            jnp.concatenate([partner_stats, stats_all], 0),
            jnp.concatenate([stats_all, partner_stats], 0),
        )
    return (rows_all, stats_all)


def attention_scores(queries, key_values, visible):
    row_count, head_count, head_dim = queries.shape
    model_width = head_count * head_dim
    key_heads = key_values[:, :model_width].reshape(-1, head_count, head_dim)
    raw_scores = jnp.einsum(
        "qhd,khd->hqk", queries, key_heads, preferred_element_type=jnp.float32
    ) * (1.0 / math.sqrt(head_dim))
    return (jnp.where(visible[None], raw_scores, masked_score), key_heads)


def weight_products(operands):
    normed_a, d_projected, attended, d_attn, normed_m, d_gate_up, mixed_act, d_mlp = operands
    grad_qkv = jnp.einsum("td,te->de", normed_a, d_projected, preferred_element_type=jnp.float32)
    grad_attn = jnp.einsum("td,te->de", attended, d_attn, preferred_element_type=jnp.float32)
    grad_in = jnp.einsum("td,tf->df", normed_m, d_gate_up, preferred_element_type=jnp.float32)
    grad_out = jnp.einsum("tf,td->fd", mixed_act, d_mlp, preferred_element_type=jnp.float32)
    return (grad_qkv, grad_attn, grad_in, grad_out)


def forward_layer(layer_in, weights, visible, cosine, sine_table, group_pos):
    w_qkv, w_attn, w_in, w_out, gain_attn, gain_mlp = weights
    row_count, model_width = layer_in.shape
    head_count = model_width // HEAD_DIM
    normed_a = normalize(layer_in, gain_attn.astype(jnp.float32)).astype(jnp.bfloat16)
    projected = jnp.dot(normed_a, w_qkv, preferred_element_type=jnp.float32)
    queries = rotate(
        projected[:, :model_width].reshape(row_count, head_count, HEAD_DIM), cosine, sine_table
    ).astype(jnp.bfloat16)
    keys_here = rotate(
        projected[:, model_width : 2 * model_width].reshape(row_count, head_count, HEAD_DIM),
        cosine,
        sine_table,
    ).reshape(row_count, model_width)
    local_keys = jnp.concatenate([keys_here, projected[:, 2 * model_width :]], 1).astype(
        jnp.bfloat16
    )
    key_values = spread_keys(local_keys, group_pos)
    scores, key_heads = attention_scores(queries, key_values, visible)
    row_peak = jnp.max(scores, -1, keepdims=True)
    log_total = row_peak + jnp.log(jnp.sum(jnp.exp(scores - row_peak), -1, keepdims=True))
    attn_probs = jnp.exp(scores - log_total).astype(jnp.bfloat16)
    value_heads = key_values[:, model_width:].reshape(-1, head_count, HEAD_DIM)
    attended = (
        jnp.einsum("hqk,khd->qhd", attn_probs, value_heads, preferred_element_type=jnp.float32)
        .reshape(row_count, model_width)
        .astype(jnp.bfloat16)
    )
    middle = layer_in + jnp.dot(attended, w_attn, preferred_element_type=jnp.float32)
    normed_m = normalize(middle, gain_mlp.astype(jnp.float32)).astype(jnp.bfloat16)
    gate_up = jnp.dot(normed_m, w_in, preferred_element_type=jnp.float32)
    mixed_act = activate(gate_up).astype(jnp.bfloat16)
    result = middle + jnp.dot(mixed_act, w_out, preferred_element_type=jnp.float32)
    return (
        result,
        (
            layer_in,
            normed_a,
            queries,
            key_values,
            log_total,
            attended,
            middle,
            normed_m,
            gate_up,
            mixed_act,
        ),
    )


def backward_layer(upstream, residuals, weights, visible, cosine, sine_table, group_pos):
    w_qkv, w_attn, w_in, w_out, gain_attn, gain_mlp = weights
    (
        layer_in,
        normed_a,
        queries,
        key_values,
        log_total,
        attended,
        middle,
        normed_m,
        gate_up,
        mixed_act,
    ) = residuals
    row_count, model_width = layer_in.shape
    head_count = model_width // HEAD_DIM
    d_mlp = upstream.astype(jnp.bfloat16)
    d_mixed = jnp.einsum("td,fd->tf", d_mlp, w_out, preferred_element_type=jnp.float32)
    unused_act, act_back = jax.vjp(activate, gate_up)
    d_gate_up = act_back(d_mixed)[0].astype(jnp.bfloat16)
    d_normed_m = jnp.einsum("tf,df->td", d_gate_up, w_in, preferred_element_type=jnp.float32)
    unused_mid, norm_back = jax.vjp(normalize, middle, gain_mlp.astype(jnp.float32))
    d_middle, d_gain_mlp = norm_back(d_normed_m)
    d_middle = upstream + d_middle
    d_attn = d_middle.astype(jnp.bfloat16)
    d_attended = jnp.einsum("te,de->td", d_attn, w_attn, preferred_element_type=jnp.float32).astype(
        jnp.bfloat16
    )
    d_heads = d_attended.reshape(row_count, head_count, HEAD_DIM)
    scores, key_heads = attention_scores(queries, key_values, visible)
    attn_probs = jnp.exp(scores - log_total)
    value_heads = key_values[:, model_width:].reshape(-1, head_count, HEAD_DIM)
    d_probs = jnp.einsum("qhd,khd->hqk", d_heads, value_heads, preferred_element_type=jnp.float32)
    row_delta = jnp.sum(attn_probs * d_probs, -1, keepdims=True)
    d_scores = (attn_probs * (d_probs - row_delta)).astype(jnp.bfloat16)
    score_scale = 1.0 / math.sqrt(HEAD_DIM)
    d_queries = (
        jnp.einsum("hqk,khd->qhd", d_scores, key_heads, preferred_element_type=jnp.float32)
        * score_scale
    )
    query_rows = jnp.concatenate([queries.reshape(row_count, model_width), d_attended], 1)
    query_stats = jnp.concatenate([log_total[:, :, 0].T, row_delta[:, :, 0].T], 1)
    rows_all, stats_all = spread_queries(query_rows, query_stats, group_pos)
    queries_all = rows_all[:, :model_width].reshape(-1, head_count, HEAD_DIM)
    d_heads_all = rows_all[:, model_width:].reshape(-1, head_count, HEAD_DIM)
    totals_all = stats_all[:, :head_count].T[:, :, None]
    deltas_all = stats_all[:, head_count:].T[:, :, None]
    own_kv = lax.dynamic_slice_in_dim(key_values, group_pos * row_count, row_count, 0)
    own_keys = own_kv[:, :model_width].reshape(row_count, head_count, HEAD_DIM)
    own_values = own_kv[:, model_width:].reshape(row_count, head_count, HEAD_DIM)
    raw_back = (
        jnp.einsum("ahd,khd->hak", queries_all, own_keys, preferred_element_type=jnp.float32)
        * score_scale
    )
    scores_back = jnp.where(visible.T[None], raw_back, masked_score)
    probs_back = jnp.exp(scores_back - totals_all)
    d_probs_back = jnp.einsum(
        "ahd,khd->hak", d_heads_all, own_values, preferred_element_type=jnp.float32
    )
    d_scores_back = (probs_back * (d_probs_back - deltas_all)).astype(jnp.bfloat16)
    d_keys = (
        jnp.einsum("hak,ahd->khd", d_scores_back, queries_all, preferred_element_type=jnp.float32)
        * score_scale
    )
    d_values = jnp.einsum(
        "hak,ahd->khd",
        probs_back.astype(jnp.bfloat16),
        d_heads_all,
        preferred_element_type=jnp.float32,
    )
    d_query_raw = unrotate(d_queries, cosine, sine_table).reshape(row_count, model_width)
    d_key_raw = unrotate(d_keys, cosine, sine_table).reshape(row_count, model_width)
    d_projected = jnp.concatenate(
        [d_query_raw, d_key_raw, d_values.reshape(row_count, model_width)], 1
    ).astype(jnp.bfloat16)
    d_normed_a = jnp.einsum("te,de->td", d_projected, w_qkv, preferred_element_type=jnp.float32)
    unused_in, first_back = jax.vjp(normalize, layer_in, gain_attn.astype(jnp.float32))
    d_layer_in, d_gain_attn = first_back(d_normed_a)
    layer_grad = d_middle + d_layer_in
    operands = (normed_a, d_projected, attended, d_attn, normed_m, d_gate_up, mixed_act, d_mlp)
    return (layer_grad, operands, (d_gain_attn, d_gain_mlp))


def on_device(
    tokens_in,
    segment_ids,
    out_grad,
    qkv_weight,
    attn_out_weight,
    mlp_in_weight,
    mlp_out_weight,
    attn_gain,
    mlp_gain,
):
    section_pos = lax.axis_index("section")
    replica = lax.axis_index("dp")
    micro_count, row_count, model_width = tokens_in.shape
    group_pos = replica % GROUP
    key_segments = spread_segments(segment_ids, group_pos)
    seq_len = key_segments.shape[1]
    query_pos = group_pos * row_count + jnp.arange(row_count)
    key_pos = jnp.arange(seq_len)
    window_reach = jnp.where(section_pos == 0, HALF_WIN, seq_len)
    in_reach = jnp.abs(query_pos[:, None] - key_pos[None, :]) <= window_reach
    log_base = jnp.where(section_pos == 0, local_log_base, global_log_base)
    cosine, sine_table = angles(query_pos, log_base, HEAD_DIM)
    shards = (
        qkv_weight[0],
        attn_out_weight[0],
        mlp_in_weight[0],
        mlp_out_weight[0],
        attn_gain[0],
        mlp_gain[0],
    )
    resident = (
        lax.all_gather(shards[0], "dp", axis=0, tiled=True),
        lax.all_gather(shards[1], "dp", axis=0, tiled=True),
        lax.all_gather(shards[2], "dp", axis=0, tiled=True),
        lax.all_gather(shards[3], "dp", axis=0, tiled=True),
        lax.all_gather(shards[4], "dp", axis=0, tiled=True),
        lax.all_gather(shards[5], "dp", axis=0, tiled=True),
    )

    def visible_for(batch_idx):
        query_seg = lax.dynamic_index_in_dim(segment_ids, batch_idx, 0, keepdims=False)
        key_seg = lax.dynamic_index_in_dim(key_segments, batch_idx, 0, keepdims=False)
        return (query_seg[:, None] == key_seg[None, :]) & in_reach

    outputs_buf = jnp.zeros((micro_count, row_count, model_width), jnp.bfloat16)
    received = jnp.zeros((row_count, model_width), jnp.bfloat16)
    saved_list = []
    for slot_index in range(micro_count + 1):
        batch_pos = slot_index - section_pos
        is_valid = (batch_pos >= 0) & (batch_pos < micro_count)
        batch_idx = jnp.clip(batch_pos, 0, micro_count - 1)
        weights = resident
        fresh_rows = lax.dynamic_index_in_dim(tokens_in, batch_idx, 0, keepdims=False)
        layer_in = jnp.where(section_pos == 0, fresh_rows, received).astype(jnp.float32)
        result, residuals = forward_layer(
            layer_in, weights, visible_for(batch_idx), cosine, sine_table, group_pos
        )
        rounded = result.astype(jnp.bfloat16)
        updated = lax.dynamic_update_index_in_dim(outputs_buf, rounded, batch_idx, 0)
        outputs_buf = jnp.where(is_valid, updated, outputs_buf)
        saved_list.append(residuals)
        if slot_index < micro_count:
            received = passed_along(rounded, "section", 1)
    stacked = jax.tree.map(lambda *pieces: jnp.stack(pieces), *saved_list)
    grads_buf = jnp.zeros((micro_count, row_count, model_width), jnp.bfloat16)
    returned = jnp.zeros((row_count, model_width), jnp.bfloat16)
    shares = tuple((jnp.zeros(shard_item.shape, jnp.float32) for shard_item in shards))
    gain_attn_total = jnp.zeros((model_width,), jnp.float32)
    gain_mlp_total = jnp.zeros((model_width,), jnp.float32)
    kept_operands = []
    for slot_index in range(micro_count + 1):
        batch_pos = slot_index - 1 + section_pos
        is_valid = (batch_pos >= 0) & (batch_pos < micro_count)
        batch_idx = jnp.clip(batch_pos, 0, micro_count - 1)
        slot_taken = batch_idx + section_pos
        residuals = jax.tree.map(
            lambda stacked_part: lax.dynamic_index_in_dim(
                stacked_part, slot_taken, 0, keepdims=False
            ),
            stacked,
        )
        weights = resident
        given_grad = lax.dynamic_index_in_dim(out_grad, batch_idx, 0, keepdims=False)
        upstream = jnp.where(section_pos == 1, given_grad, returned).astype(jnp.float32)
        layer_grad, operands, gain_grads = backward_layer(
            upstream, residuals, weights, visible_for(batch_idx), cosine, sine_table, group_pos
        )
        valid_scale = is_valid.astype(jnp.float32)
        sent_grad = layer_grad.astype(jnp.bfloat16)
        updated = lax.dynamic_update_index_in_dim(grads_buf, sent_grad, batch_idx, 0)
        grads_buf = jnp.where(is_valid, updated, grads_buf)
        gain_attn_total = gain_attn_total + gain_grads[0] * valid_scale
        gain_mlp_total = gain_mlp_total + gain_grads[1] * valid_scale
        masked_ops = tuple(
            (
                (
                    op_item
                    if op_index % 2 == 0
                    else jnp.where(is_valid, op_item, jnp.zeros_like(op_item))
                )
                for op_index, op_item in enumerate(operands)
            )
        )
        kept_operands.append(masked_ops)
        if slot_index < micro_count:
            returned = passed_along(sent_grad, "section", -1)
    joined = tuple(
        (
            jnp.concatenate([slot_ops[op_index] for slot_ops in kept_operands], 0)
            for op_index in range(8)
        )
    )
    totals = weight_products(joined) + (gain_attn_total, gain_mlp_total)
    shares = lax.psum_scatter(totals, "dp", scatter_dimension=0, tiled=True)
    return (
        outputs_buf[None],
        grads_buf[None],
        shares[0][None],
        shares[1][None],
        shares[2][None],
        shares[3][None],
        shares[4][None],
        shares[5][None],
    )


def solution(mesh):
    in_specs = (
        P(None, "dp", None),
        P(None, "dp"),
        P(None, "dp", None),
        P("section", "dp", None),
        P("section", "dp", None),
        P("section", "dp", None),
        P("section", "dp", None),
        P("section", "dp"),
        P("section", "dp"),
    )
    out_specs = (
        P("section", None, "dp", None),
        P("section", None, "dp", None),
        P("section", "dp", None),
        P("section", "dp", None),
        P("section", "dp", None),
        P("section", "dp", None),
        P("section", "dp"),
        P("section", "dp"),
    )
    return jax.shard_map(
        on_device, mesh=mesh, in_specs=in_specs, out_specs=out_specs, check_vma=False
    )
```

profile of v0, /device:TPU:0, one launch (start us, length us, event | category | flops | bytes accessed | tf_op | source)
XLA Modules:
  0.0 1257.9 jit_solution(8325390348457825665)
XLA Ops:
  13.1 35.2 %all-reduce.11 = (bf16[768]{0:T(1024)(128)(2,1)S(1)}, bf16[768]{0:T(1024)(128)(2,1)S(1)}) all-reduce(bf16[768]{0:T(1024)(128)(2,1)S(1)} %dynamic-update-slice.8, bf16[768]{0:T(1024)(128)(2,1)S(1)} %dynamic-update-slice.9), channel_id=2, replica_groups=mesh['section'=2,'dp'=16] {'dp'}, use_global_device_ids=true, to_apply=%add.6 | all-reduce | flops 1536 | bytes 6144
  51.7 8.3 all-gather.11.cloned.1.call-done
  66.0 11.4 collective-permute-done.1
  79.7 22.4 %collective-permute-done.2 = bf16[256,1536]{1,0:T(8,128)(2,1)S(1)} collective-permute-done((bf16[256,1536]{1,0:T(8,128)(2,1)S(1)}, bf16[256,1536]{1,0:T(8,128)(2,1)S(1)}, u32[]{:S(2)}, u32[]{:S(2)}) %collective-permute-start.2) | collective-permute-done | bytes 786464 | tf_op jit(solution)/shard_map/ppermute | solution.py:19
  110.1 30.4 %collective-permute-done.6 = s32[2,256]{1,0:T(2,128)S(1)} collective-permute-done((s32[2,256]{1,0:T(2,128)S(1)}, s32[2,256]{1,0:T(2,128)S(1)}, u32[]{:S(2)}, u32[]{:S(2)}) %collective-permute-start.6) | collective-permute-done | bytes 2080 | tf_op jit(solution)/shard_map/ppermute | solution.py:19
  144.0 36.4 %collective-permute-done.7 = s32[2,512]{1,0:T(2,128)S(1)} collective-permute-done((s32[2,512]{1,0:T(2,128)S(1)}, s32[2,512]{1,0:T(2,128)S(1)}, u32[]{:S(2)}, u32[]{:S(2)}) %collective-permute-start.7) | collective-permute-done | bytes 4128 | tf_op jit(solution)/shard_map/ppermute | solution.py:19
  197.7 7.4 all-gather.15.cloned.1.call-done
  208.8 37.8 %all-gather.17.cloned.1.call-done = bf16[1,1152,768]{2,1,0:T(8,128)(2,1)} async-done(((bf16[1,72,768]{2,1,0:T(8,128)(2,1)}), bf16[1,1152,768]{2,1,0:T(8,128)(2,1)}) %all-gather.17.cloned.1.call-update) | async-done | bytes 1769488 | tf_op jit(solution)/shard_map/all_gather | solution.py:296
  249.4 3.9 collective-permute-start.8
  271.9 10.6 collective-permute-done.10
  283.1 18.3 %collective-permute-done.11 = bf16[256,1536]{1,0:T(8,128)(2,1)S(1)} collective-permute-done((bf16[256,1536]{1,0:T(8,128)(2,1)S(1)}, bf16[256,1536]{1,0:T(8,128)(2,1)S(1)}, u32[]{:S(2)}, u32[]{:S(2)}) %collective-permute-start.11) | collective-permute-done | bytes 786464 | tf_op jit(solution)/shard_map/ppermute | solution.py:19
  309.3 63.4 %collective-permute-done.12 = bf16[512,1536]{1,0:T(8,128)(2,1)} collective-permute-done((bf16[512,1536]{1,0:T(8,128)(2,1)}, bf16[512,1536]{1,0:T(8,128)(2,1)}, u32[]{:S(2)}, u32[]{:S(2)}) %collective-permute-start.12) | collective-permute-done | bytes 1572896 | tf_op jit(solution)/shard_map/ppermute | solution.py:19
  390.5 4.4 collective-permute-start.13
  419.4 6.0 collective-permute-done.15
  427.7 4.7 maximum_select_fusion.3
  434.3 4.5 maximum_select_fusion.4
  440.6 6.2 collective-permute-done.16
  465.7 54.1 %collective-permute-done.17 = bf16[512,1536]{1,0:T(8,128)(2,1)} collective-permute-done((bf16[512,1536]{1,0:T(8,128)(2,1)}, bf16[512,1536]{1,0:T(8,128)(2,1)}, u32[]{:S(2)}, u32[]{:S(2)}) %collective-permute-start.17) | collective-permute-done | bytes 1572896 | tf_op jit(solution)/shard_map/ppermute | solution.py:19
  552.0 4.0 dynamic-slice_bitcast_fusion
  561.0 3.8 fusion.415
  580.3 14.3 %collective-permute-done.20 = bf16[256,1536]{1,0:T(8,128)(2,1)S(1)} collective-permute-done((bf16[256,1536]{1,0:T(8,128)(2,1)S(1)}, bf16[256,1536]{1,0:T(8,128)(2,1)S(1)}, u32[]{:S(2)}, u32[]{:S(2)}) %collective-permute-start.20) | collective-permute-done | bytes 786464 | tf_op jit(solution)/shard_map/ppermute | solution.py:19
  607.1 24.6 %collective-permute-done.24 = f32[256,24]{0,1:T(8,128)S(1)} collective-permute-done((f32[256,24]{0,1:T(8,128)S(1)}, f32[256,24]{0,1:T(8,128)S(1)}, u32[]{:S(2)}, u32[]{:S(2)}) %collective-permute-start.24) | collective-permute-done | bytes 24608 | tf_op jit(solution)/shard_map/ppermute | solution.py:19
  639.3 29.8 %collective-permute-done.25 = f32[512,24]{0,1:T(8,128)} collective-permute-done((f32[512,24]{0,1:T(8,128)}, f32[512,24]{0,1:T(8,128)}, u32[]{:S(2)}, u32[]{:S(2)}) %collective-permute-start.25) | collective-permute-done | bytes 49184 | tf_op jit(solution)/shard_map/ppermute | solution.py:19
  687.1 5.2 fusion.86
  692.4 4.6 broadcast_multiply_fusion.5
  709.4 5.4 collective-permute-done.26
  725.1 9.9 collective-permute-done.28
  737.5 3.7 fusion.413
  746.6 3.7 fusion.287
  752.1 5.2 multiply_reduce_fusion.1
  773.8 23.4 %collective-permute-done.33 = f32[256,24]{0,1:T(8,128)} collective-permute-done((f32[256,24]{0,1:T(8,128)}, f32[256,24]{0,1:T(8,128)}, u32[]{:S(2)}, u32[]{:S(2)}) %collective-permute-start.33) | collective-permute-done | bytes 24608 | tf_op jit(solution)/shard_map/ppermute | solution.py:19
  802.0 31.4 %collective-permute-done.34 = f32[512,24]{0,1:T(8,128)S(1)} collective-permute-done((f32[512,24]{0,1:T(8,128)S(1)}, f32[512,24]{0,1:T(8,128)S(1)}, u32[]{:S(2)}, u32[]{:S(2)}) %collective-permute-start.34) | collective-permute-done | bytes 49184 | tf_op jit(solution)/shard_map/ppermute | solution.py:19
  850.0 5.2 fusion.85
  855.3 4.6 broadcast_multiply_fusion.3
  871.1 4.9 collective-permute-done.35
  896.0 4.1 fusion.168
  913.4 3.7 fusion.411
  929.1 3.8 fusion.285
  934.6 5.2 multiply_reduce_fusion
  940.0 13.8 %collective-permute-done.38 = bf16[256,1536]{1,0:T(8,128)(2,1)} collective-permute-done((bf16[256,1536]{1,0:T(8,128)(2,1)}, bf16[256,1536]{1,0:T(8,128)(2,1)}, u32[]{:S(2)}, u32[]{:S(2)}) %collective-permute-start.38) | collective-permute-done | bytes 786464 | tf_op jit(solution)/shard_map/ppermute | solution.py:19
  963.9 34.9 %collective-permute-done.42 = f32[256,24]{0,1:T(8,128)S(1)} collective-permute-done((f32[256,24]{0,1:T(8,128)S(1)}, f32[256,24]{0,1:T(8,128)S(1)}, u32[]{:S(2)}, u32[]{:S(2)}) %collective-permute-start.42) | collective-permute-done | bytes 24608 | tf_op jit(solution)/shard_map/ppermute | solution.py:19
  1000.4 42.1 %collective-permute-done.43 = f32[512,24]{0,1:T(8,128)S(1)} collective-permute-done((f32[512,24]{0,1:T(8,128)S(1)}, f32[512,24]{0,1:T(8,128)S(1)}, u32[]{:S(2)}, u32[]{:S(2)}) %collective-permute-start.43) | collective-permute-done | bytes 49184 | tf_op jit(solution)/shard_map/ppermute | solution.py:19
  1057.3 5.2 fusion.84
  1062.5 4.6 broadcast_multiply_fusion.1
  1072.5 5.5 fusion.162
  1087.2 31.5 %all-reduce.10 = (f32[768]{0:T(1024)S(1)}, f32[768]{0:T(1024)S(1)}) all-reduce(f32[768]{0:T(1024)S(1)} %multiply_add_fusion.4, f32[768]{0:T(1024)S(1)} %multiply_add_fusion.3), channel_id=12, replica_groups=mesh['section'=2,'dp'=16] {'dp'}, use_global_device_ids=true, to_apply=%region_52.53.clone | all-reduce | flops 1536 | bytes 12288
  1123.6 32.7 %reduce-scatter.9.cloned.1.call-done = f32[48,2304]{1,0:T(8,128)} async-done(((f32[768,2304]{1,0:T(8,128)}), f32[48,2304]{1,0:T(8,128)}) %reduce-scatter.9.cloned.1.call-update) | async-done | bytes 442384 | tf_op jit(solution)/shard_map/reduce_scatter | solution.py:375
  1156.4 94.2 %reduce-scatter.5.cloned.1.call-done = f32[48,2304]{1,0:T(8,128)} async-done(((f32[768,2304]{1,0:T(8,128)}), f32[48,2304]{1,0:T(8,128)}) %reduce-scatter.5.cloned.1.call-update) | async-done | bytes 442384 | tf_op jit(solution)/shard_map/reduce_scatter | solution.py:375
  (790 shorter events, 408.4 us)
Async XLA Ops:
  7.2 52.8 %all-gather.11.cloned.1.call-start = ((), (), s32[]{:S(2)}) async-start(), calls=%async_computation.8 | async-start | bytes 3760128 | tf_op jit(solution)/shard_map/all_gather | solution.py:293
  7.9 187.8 %all-gather.13.cloned.1.call-start = ((), (), s32[]{:S(2)}) async-start(), calls=%async_computation.9 | async-start | bytes 1253376 | tf_op jit(solution)/shard_map/all_gather | solution.py:294
  8.6 196.5 %all-gather.15.cloned.1.call-start = ((), (), s32[]{:S(2)}) async-start(), calls=%async_computation.10 | async-start | bytes 3760128 | tf_op jit(solution)/shard_map/all_gather | solution.py:295
  9.4 237.2 %all-gather.17.cloned.1.call-start = ((), (), s32[]{:S(2)}) async-start(), calls=%async_computation.11 | async-start | bytes 1880064 | tf_op jit(solution)/shard_map/all_gather | solution.py:296
  63.7 1.5 collective-permute-start
  65.3 12.1 collective-permute-start.1
  77.6 24.5 %collective-permute-start.2 = (bf16[256,1536]{1,0:T(8,128)(2,1)S(1)}, bf16[256,1536]{1,0:T(8,128)(2,1)S(1)}, u32[]{:S(2)}, u32[]{:S(2)}) collective-permute-start(bf16[256,1536]{1,0:T(8,128)(2,1)S(1)} %maximum_select_fusion.15), channel_id=1, source_target_pairs={{0,4},{1,5},{2,6},{3,7},{4,0},{5,1},{6,2},{7,3},{8,12},{9,13},{10,... | collective-permute-start | bytes 2359304 | tf_op jit(solution)/shard_map/ppermute | solution.py:19
  102.7 81.2 %collective-permute-start.3 = (bf16[512,1536]{1,0:T(8,128)(2,1)S(1)}, bf16[512,1536]{1,0:T(8,128)(2,1)}, u32[]{:S(2)}, u32[]{:S(2)}) collective-permute-start(bf16[512,1536]{1,0:T(8,128)(2,1)S(1)} %maximum_select_fusion.9), channel_id=1, source_target_pairs={{0,8},{1,9},{2,10},{3,11},{4,12},{5,13},{6,14},{7,15},{8,0},{9,1},... | collective-permute-start | bytes 4718600 | tf_op jit(solution)/shard_map/ppermute | solution.py:19
  105.5 3.6 collective-permute-start.5
  109.1 31.5 %collective-permute-start.6 = (s32[2,256]{1,0:T(2,128)S(1)}, s32[2,256]{1,0:T(2,128)S(1)}, u32[]{:S(2)}, u32[]{:S(2)}) collective-permute-start(s32[2,256]{1,0:T(2,128)S(1)} %add_select_fusion.2), channel_id=1, source_target_pairs={{0,4},{1,5},{2,6},{3,7},{4,0},{5,1},{6,2},{7,3},{8,12},{9,13},{10,... | collective-permute-start | bytes 6152 | tf_op jit(solution)/shard_map/ppermute | solution.py:19
  110.1 1013.6 %reduce-scatter.7.cloned.1.call-start = ((), (), s32[]{:S(2)}) async-start(), calls=%async_computation.5 | async-start | bytes 2506752 | tf_op jit(solution)/shard_map/reduce_scatter | solution.py:375
  140.6 39.9 %collective-permute-start.7 = (s32[2,512]{1,0:T(2,128)S(1)}, s32[2,512]{1,0:T(2,128)S(1)}, u32[]{:S(2)}, u32[]{:S(2)}) collective-permute-start(s32[2,512]{1,0:T(2,128)S(1)} %add_select_fusion.1), channel_id=1, source_target_pairs={{0,8},{1,9},{2,10},{3,11},{4,12},{5,13},{6,14},{7,15},{8,0},{9,1},... | collective-permute-start | bytes 12296 | tf_op jit(solution)/shard_map/ppermute | solution.py:19
  249.4 5.8 collective-permute-start.8
  268.7 1.5 collective-permute-start.9
  271.2 11.2 collective-permute-start.10
  282.6 18.8 %collective-permute-start.11 = (bf16[256,1536]{1,0:T(8,128)(2,1)S(1)}, bf16[256,1536]{1,0:T(8,128)(2,1)S(1)}, u32[]{:S(2)}, u32[]{:S(2)}) collective-permute-start(bf16[256,1536]{1,0:T(8,128)(2,1)S(1)} %maximum_select_fusion.16), channel_id=1, source_target_pairs={{0,4},{1,5},{2,6},{3,7},{4,0},{5,1},{6,2},{7,3},{8,12},{9,13},{10,... | collective-permute-start | bytes 2359304 | tf_op jit(solution)/shard_map/ppermute | solution.py:19
  303.2 69.5 %collective-permute-start.12 = (bf16[512,1536]{1,0:T(8,128)(2,1)}, bf16[512,1536]{1,0:T(8,128)(2,1)}, u32[]{:S(2)}, u32[]{:S(2)}) collective-permute-start(bf16[512,1536]{1,0:T(8,128)(2,1)} %maximum_select_fusion.10), channel_id=1, source_target_pairs={{0,8},{1,9},{2,10},{3,11},{4,12},{5,13},{6,14},{7,15},{8,0},{9,1},... | collective-permute-start | bytes 4718600 | tf_op jit(solution)/shard_map/ppermute | solution.py:19
  390.5 6.6 collective-permute-start.13
  413.8 11.5 collective-permute-start.15
  427.7 19.1 %collective-permute-start.16 = (bf16[256,1536]{1,0:T(8,128)(2,1)}, bf16[256,1536]{1,0:T(8,128)(2,1)}, u32[]{:S(2)}, u32[]{:S(2)}) collective-permute-start(bf16[256,1536]{1,0:T(8,128)(2,1)} %maximum_select_fusion.17), channel_id=1, source_target_pairs={{0,4},{1,5},{2,6},{3,7},{4,0},{5,1},{6,2},{7,3},{8,12},{9,13},{10,... | collective-permute-start | bytes 2359304 | tf_op jit(solution)/shard_map/ppermute | solution.py:19
  450.2 69.6 %collective-permute-start.17 = (bf16[512,1536]{1,0:T(8,128)(2,1)}, bf16[512,1536]{1,0:T(8,128)(2,1)}, u32[]{:S(2)}, u32[]{:S(2)}) collective-permute-start(bf16[512,1536]{1,0:T(8,128)(2,1)} %maximum_select_fusion.11), channel_id=1, source_target_pairs={{0,8},{1,9},{2,10},{3,11},{4,12},{5,13},{6,14},{7,15},{8,0},{9,1},... | collective-permute-start | bytes 4718600 | tf_op jit(solution)/shard_map/ppermute | solution.py:19
  546.0 12.6 collective-permute-start.18
  560.5 12.7 %collective-permute-start.19 = (bf16[128,1536]{1,0:T(8,128)(2,1)}, bf16[128,1536]{1,0:T(8,128)(2,1)}, u32[]{:S(2)}, u32[]{:S(2)}) collective-permute-start(bf16[128,1536]{1,0:T(8,128)(2,1)} %maximum_select_fusion.24), channel_id=1, source_target_pairs={{0,2},{1,3},{2,0},{3,1},{4,6},{5,7},{6,4},{7,5},{8,10},{9,11},{10,... | collective-permute-start | bytes 1179656 | tf_op jit(solution)/shard_map/ppermute | solution.py:19
  574.9 19.7 %collective-permute-start.20 = (bf16[256,1536]{1,0:T(8,128)(2,1)S(1)}, bf16[256,1536]{1,0:T(8,128)(2,1)S(1)}, u32[]{:S(2)}, u32[]{:S(2)}) collective-permute-start(bf16[256,1536]{1,0:T(8,128)(2,1)S(1)} %maximum_select_fusion.18), channel_id=1, source_target_pairs={{0,4},{1,5},{2,6},{3,7},{4,0},{5,1},{6,2},{7,3},{8,12},{9,13},{10,... | collective-permute-start | bytes 2359304 | tf_op jit(solution)/shard_map/ppermute | solution.py:19
  580.0 17.9 %collective-permute-start.22 = (f32[64,24]{0,1:T(8,128)S(1)}, f32[64,24]{0,1:T(8,128)S(1)}, u32[]{:S(2)}, u32[]{:S(2)}) collective-permute-start(f32[64,24]{0,1:T(8,128)S(1)} %pad_maximum_fusion.23), channel_id=1, source_target_pairs={{0,1},{1,0},{2,3},{3,2},{4,5},{5,4},{6,7},{7,6},{8,9},{9,8},{10,11... | collective-permute-start | bytes 18440 | tf_op jit(solution)/shard_map/ppermute | solution.py:19
  596.4 74.3 %collective-permute-start.21 = (bf16[512,1536]{1,0:T(8,128)(2,1)}, bf16[512,1536]{1,0:T(8,128)(2,1)}, u32[]{:S(2)}, u32[]{:S(2)}) collective-permute-start(bf16[512,1536]{1,0:T(8,128)(2,1)} %maximum_select_fusion.12), channel_id=1, source_target_pairs={{0,8},{1,9},{2,10},{3,11},{4,12},{5,13},{6,14},{7,15},{8,0},{9,1},... | collective-permute-start | bytes 4718600 | tf_op jit(solution)/shard_map/ppermute | solution.py:19
  598.5 4.0 collective-permute-start.23
  603.4 28.3 %collective-permute-start.24 = (f32[256,24]{0,1:T(8,128)S(1)}, f32[256,24]{0,1:T(8,128)S(1)}, u32[]{:S(2)}, u32[]{:S(2)}) collective-permute-start(f32[256,24]{0,1:T(8,128)S(1)} %maximum_select_fusion.33), channel_id=1, source_target_pairs={{0,4},{1,5},{2,6},{3,7},{4,0},{5,1},{6,2},{7,3},{8,12},{9,13},{10,... | collective-permute-start | bytes 73736 | tf_op jit(solution)/shard_map/ppermute | solution.py:19
  632.3 36.8 %collective-permute-start.25 = (f32[512,24]{0,1:T(8,128)}, f32[512,24]{0,1:T(8,128)}, u32[]{:S(2)}, u32[]{:S(2)}) collective-permute-start(f32[512,24]{0,1:T(8,128)} %maximum_select_fusion.30), channel_id=1, source_target_pairs={{0,8},{1,9},{2,10},{3,11},{4,12},{5,13},{6,14},{7,15},{8,0},{9,1},... | collective-permute-start | bytes 147464 | tf_op jit(solution)/shard_map/ppermute | solution.py:19
  708.1 6.7 collective-permute-start.26
  723.6 11.5 collective-permute-start.28
  737.5 19.9 %collective-permute-start.29 = (bf16[256,1536]{1,0:T(8,128)(2,1)}, bf16[256,1536]{1,0:T(8,128)(2,1)}, u32[]{:S(2)}, u32[]{:S(2)}) collective-permute-start(bf16[256,1536]{1,0:T(8,128)(2,1)} %maximum_select_fusion.19), channel_id=1, source_target_pairs={{0,4},{1,5},{2,6},{3,7},{4,0},{5,1},{6,2},{7,3},{8,12},{9,13},{10,... | collective-permute-start | bytes 2359304 | tf_op jit(solution)/shard_map/ppermute | solution.py:19
  760.8 73.2 %collective-permute-start.30 = (bf16[512,1536]{1,0:T(8,128)(2,1)}, bf16[512,1536]{1,0:T(8,128)(2,1)}, u32[]{:S(2)}, u32[]{:S(2)}) collective-permute-start(bf16[512,1536]{1,0:T(8,128)(2,1)} %maximum_select_fusion.13), channel_id=1, source_target_pairs={{0,8},{1,9},{2,10},{3,11},{4,12},{5,13},{6,14},{7,15},{8,0},{9,1},... | collective-permute-start | bytes 4718600 | tf_op jit(solution)/shard_map/ppermute | solution.py:19
  764.9 3.7 collective-permute-start.32
  769.2 28.0 %collective-permute-start.33 = (f32[256,24]{0,1:T(8,128)}, f32[256,24]{0,1:T(8,128)}, u32[]{:S(2)}, u32[]{:S(2)}) collective-permute-start(f32[256,24]{0,1:T(8,128)} %maximum_select_fusion.34), channel_id=1, source_target_pairs={{0,4},{1,5},{2,6},{3,7},{4,0},{5,1},{6,2},{7,3},{8,12},{9,13},{10,... | collective-permute-start | bytes 73736 | tf_op jit(solution)/shard_map/ppermute | solution.py:19
  798.0 35.4 %collective-permute-start.34 = (f32[512,24]{0,1:T(8,128)S(1)}, f32[512,24]{0,1:T(8,128)S(1)}, u32[]{:S(2)}, u32[]{:S(2)}) collective-permute-start(f32[512,24]{0,1:T(8,128)S(1)} %maximum_select_fusion.31), channel_id=1, source_target_pairs={{0,8},{1,9},{2,10},{3,11},{4,12},{5,13},{6,14},{7,15},{8,0},{9,1},... | collective-permute-start | bytes 147464 | tf_op jit(solution)/shard_map/ppermute | solution.py:19
  869.5 6.5 collective-permute-start.35
  884.6 239.1 %reduce-scatter.11.cloned.1.call-start = ((), (), s32[]{:S(2)}) async-start(), calls=%async_computation.7 | async-start | bytes 3760128 | tf_op jit(solution)/shard_map/reduce_scatter | solution.py:375
  892.5 263.9 %reduce-scatter.9.cloned.1.call-start = ((), (), s32[]{:S(2)}) async-start(), calls=%async_computation.6 | async-start | bytes 7520256 | tf_op jit(solution)/shard_map/reduce_scatter | solution.py:375
  900.1 350.4 %reduce-scatter.5.cloned.1.call-start = ((), (), s32[]{:S(2)}) async-start(), calls=%async_computation.4 | async-start | bytes 7520256 | tf_op jit(solution)/shard_map/reduce_scatter | solution.py:375
  905.0 1.7 collective-permute-start.36
  908.5 18.1 %collective-permute-start.37 = (bf16[128,1536]{1,0:T(8,128)(2,1)}, bf16[128,1536]{1,0:T(8,128)(2,1)}, u32[]{:S(2)}, u32[]{:S(2)}) collective-permute-start(bf16[128,1536]{1,0:T(8,128)(2,1)} %maximum_select_fusion.26), channel_id=1, source_target_pairs={{0,2},{1,3},{2,0},{3,1},{4,6},{5,7},{6,4},{7,5},{8,10},{9,11},{10,... | collective-permute-start | bytes 1179656 | tf_op jit(solution)/shard_map/ppermute | solution.py:19
  929.1 24.7 %collective-permute-start.38 = (bf16[256,1536]{1,0:T(8,128)(2,1)}, bf16[256,1536]{1,0:T(8,128)(2,1)}, u32[]{:S(2)}, u32[]{:S(2)}) collective-permute-start(bf16[256,1536]{1,0:T(8,128)(2,1)} %maximum_select_fusion.20), channel_id=1, source_target_pairs={{0,4},{1,5},{2,6},{3,7},{4,0},{5,1},{6,2},{7,3},{8,12},{9,13},{10,... | collective-permute-start | bytes 2359304 | tf_op jit(solution)/shard_map/ppermute | solution.py:19
  939.9 19.5 %collective-permute-start.40 = (f32[64,24]{0,1:T(8,128)S(1)}, f32[64,24]{0,1:T(8,128)S(1)}, u32[]{:S(2)}, u32[]{:S(2)}) collective-permute-start(f32[64,24]{0,1:T(8,128)S(1)} %pad_maximum_fusion.25), channel_id=1, source_target_pairs={{0,1},{1,0},{2,3},{3,2},{4,5},{5,4},{6,7},{7,6},{8,9},{9,8},{10,11... | collective-permute-start | bytes 18440 | tf_op jit(solution)/shard_map/ppermute | solution.py:19
  956.2 87.0 %collective-permute-start.39 = (bf16[512,1536]{1,0:T(8,128)(2,1)S(1)}, bf16[512,1536]{1,0:T(8,128)(2,1)S(1)}, u32[]{:S(2)}, u32[]{:S(2)}) collective-permute-start(bf16[512,1536]{1,0:T(8,128)(2,1)S(1)} %maximum_select_fusion.14), channel_id=1, source_target_pairs={{0,8},{1,9},{2,10},{3,11},{4,12},{5,13},{6,14},{7,15},{8,0},{9,1},... | collective-permute-start | bytes 4718600 | tf_op jit(solution)/shard_map/ppermute | solution.py:19
  959.5 3.7 collective-permute-start.41
  963.2 35.7 %collective-permute-start.42 = (f32[256,24]{0,1:T(8,128)S(1)}, f32[256,24]{0,1:T(8,128)S(1)}, u32[]{:S(2)}, u32[]{:S(2)}) collective-permute-start(f32[256,24]{0,1:T(8,128)S(1)} %maximum_select_fusion.35), channel_id=1, source_target_pairs={{0,4},{1,5},{2,6},{3,7},{4,0},{5,1},{6,2},{7,3},{8,12},{9,13},{10,... | collective-permute-start | bytes 73736 | tf_op jit(solution)/shard_map/ppermute | solution.py:19
  998.8 43.7 %collective-permute-start.43 = (f32[512,24]{0,1:T(8,128)S(1)}, f32[512,24]{0,1:T(8,128)S(1)}, u32[]{:S(2)}, u32[]{:S(2)}) collective-permute-start(f32[512,24]{0,1:T(8,128)S(1)} %maximum_select_fusion.32), channel_id=1, source_target_pairs={{0,8},{1,9},{2,10},{3,11},{4,12},{5,13},{6,14},{7,15},{8,0},{9,1},... | collective-permute-start | bytes 147464 | tf_op jit(solution)/shard_map/ppermute | solution.py:19
  (200 other events, 2776.4 us)
Sparse Core Ops, SparseCore 0:
  10.3 49.6 all-gather.10
  62.3 38.4 all-gather.12
  103.0 102.1 all-gather.14
  207.2 39.3 all-gather.16
  884.7 70.2 reduce-scatter.6
  959.8 101.8 reduce-scatter.10
  1066.8 89.5 reduce-scatter.8
  1160.9 89.5 reduce-scatter.4
where the time goes:
time: 1270 us; the launch traced here: 1260 us
  waiting for transfers between devices  697 us (55%)
  local copies, waits for them, and re-layouts  156 us (12%)
  other arithmetic  142 us (11%)
  matrix products  129 us (10%)
  blocking collectives  66.7 us (5%)
  starting transfers between devices  48.2 us (4%)
  between operations  19 us (1%)
    ppermute x40, waiting for transfers between devices, from_partner(): lax.ppermute(x, axis, [(i, i ^ 1 << apart) for i in range(lax.axis_size(a...  500 us
    reduce_scatter x4, waiting for transfers between devices, on_device(): shares = lax.psum_scatter(totals, 'dp', scatter_dimension=0, tiled=True)  127 us
    unnamed x2, blocking collectives  66.7 us
    all_gather x1, waiting for transfers between devices, on_device(): lax.all_gather(shards[3], 'dp', axis=0, tiled=True)  37.8 us
    ppermute x40, starting transfers between devices, from_partner(): lax.ppermute(x, axis, [(i, i ^ 1 << apart) for i in range(lax.axis_size(a...  36.6 us
    select_n x15, other arithmetic, spread_keys(): jnp.where(upper_flag(group_pos, bit_index), jnp.concatenate([partner, gat...  32.7 us
    slice x12, local copies, waits for them, and re-layouts, attention_scores(): key_heads = key_values[:, :model_width].reshape(-1, head_count, head_dim)  29.9 us
    select_n x12, other arithmetic, spread_queries(): jnp.where(is_upper, jnp.concatenate([partner_rows, rows_all], 0), jnp.con...  26.2 us
  transfers between devices with their start and end apart: 52, of which 39 were waited for; matrix products, arithmetic and copies ran while one was open for 19% of the time, Pallas kernels for 0%

commit v1 on v0

v1 whole, which is shorter than its diff:
```python
import math

import jax
import jax.numpy as jnp
from jax import lax
from jax.sharding import PartitionSpec as P

HEAD_DIM = 64
GROUP = 16
HALF_WIN = 64
HEADS = 12

local_log_base = math.log(10000.0)
global_log_base = math.log(160000.0)
masked_score = -1e30
SCALE = 1.0 / math.sqrt(HEAD_DIM)
BF = jnp.bfloat16
F32 = jnp.float32


def dot(left, right):
    return jnp.dot(left, right, preferred_element_type=F32)


def dot_bt(left, right):
    return lax.dot_general(left, right, (((1,), (1,)), ((), ())), preferred_element_type=F32)


def dot_at(left, right):
    return lax.dot_general(left, right, (((0,), (0,)), ((), ())), preferred_element_type=F32)


def moments(values):
    center = values - jnp.mean(values, -1, keepdims=True)
    scale = lax.rsqrt(jnp.mean(center * center, -1, keepdims=True) + 1e-05)
    return center * scale, scale


def norm_back(grad_out, gain_row, xhat, scale):
    scaled = grad_out * gain_row
    mean_grad = jnp.mean(scaled, -1, keepdims=True)
    mean_dot = jnp.mean(scaled * xhat, -1, keepdims=True)
    return (scaled - mean_grad - xhat * mean_dot) * scale


def angles(positions, log_base):
    half_dim = HEAD_DIM // 2
    fraction = (2 * jnp.arange(half_dim)).astype(F32) / HEAD_DIM
    inverse = jnp.exp(-fraction * log_base)
    table = positions.astype(F32)[:, None] * inverse[None, :]
    table = jnp.concatenate([table, table], -1)
    cosine, sine = jnp.cos(table), jnp.sin(table)
    return jnp.tile(cosine, (2, 1))[:, None, :], jnp.tile(sine, (2, 1))[:, None, :]


def rotate(values, tables):
    cosine, sine = tables
    heads = values.reshape(values.shape[0], HEADS, HEAD_DIM)
    half = HEAD_DIM // 2
    turned = jnp.concatenate([-heads[..., half:], heads[..., :half]], -1)
    return (heads * cosine + turned * sine).reshape(values.shape)


def unrotate(grads, tables):
    cosine, sine = tables
    heads = grads.reshape(grads.shape[0], HEADS, HEAD_DIM)
    half = HEAD_DIM // 2
    scaled = heads * sine
    turned = jnp.concatenate([scaled[..., half:], -scaled[..., :half]], -1)
    return (heads * cosine + turned).reshape(grads.shape)


def project(layer_in, weights, tables):
    width = layer_in.shape[1]
    xhat, scale = moments(layer_in)
    normed = (xhat * weights["gain_attn"]).astype(BF)
    projected = dot(normed, weights["qkv"])
    queries = rotate(projected[:, :width], tables).astype(BF)
    keys = rotate(projected[:, width : 2 * width], tables).astype(BF)
    values = projected[:, 2 * width :].astype(BF)
    return normed, queries, keys, values


def finish_forward(layer_in, attended, weights):
    middle = layer_in + dot(attended, weights["attn"])
    xhat, scale = moments(middle)
    normed = (xhat * weights["gain_mlp"]).astype(BF)
    gate_up = dot(normed, weights["mlp_in"])
    half = gate_up.shape[1] // 2
    gate, up = gate_up[:, :half], gate_up[:, half:]
    mixed = (jax.nn.gelu(gate, approximate=False) * up).astype(BF)
    result = (middle + dot(mixed, weights["mlp_out"])).astype(BF)
    return result, (normed, gate_up, mixed, xhat, scale)


def start_backward(upstream, saved, weights):
    normed, gate_up, mixed, xhat, scale = saved
    d_mlp = upstream.astype(BF)
    d_mixed = dot_bt(d_mlp, weights["mlp_out"])
    half = gate_up.shape[1] // 2
    gate, up = gate_up[:, :half], gate_up[:, half:]
    cdf = 0.5 * (1.0 + lax.erf(gate * math.sqrt(0.5)))
    density = jnp.exp(-0.5 * gate * gate) * (1.0 / math.sqrt(2.0 * math.pi))
    d_gate = d_mixed * up * (cdf + gate * density)
    d_up = d_mixed * gate * cdf
    d_gate_up = jnp.concatenate([d_gate, d_up], 1).astype(BF)
    d_normed = dot_bt(d_gate_up, weights["mlp_in"])
    gain_grad = jnp.sum(d_normed * xhat, 0)
    d_middle = upstream + norm_back(d_normed, weights["gain_mlp"], xhat, scale)
    d_attn = d_middle.astype(BF)
    d_attended = dot_bt(d_attn, weights["attn"]).astype(BF)
    return d_middle, d_attended, (normed, d_gate_up, mixed, d_mlp, d_attn), gain_grad


def finish_backward(d_middle, d_projected, layer_in, weights):
    d_normed = dot_bt(d_projected, weights["qkv"])
    xhat, scale = moments(layer_in)
    gain_grad = jnp.sum(d_normed * xhat, 0)
    grad = d_middle + norm_back(d_normed, weights["gain_attn"], xhat, scale)
    return grad.astype(BF), gain_grad


def neighbours(count, step):
    return [
        (i, i + step)
        for i in range(count)
        if 0 <= i + step < count and i // GROUP == (i + step) // GROUP
    ]


def with_halo(rows, count):
    before = lax.ppermute(rows, "dp", neighbours(count, 1))
    after = lax.ppermute(rows, "dp", neighbours(count, -1))
    return jnp.concatenate([before, rows, after], 1)


def local_scores(queries, keys, visible):
    raw = jnp.einsum("bqhd,bkhd->bhqk", queries, keys, preferred_element_type=F32) * SCALE
    scores = jnp.where(visible[:, None], raw, masked_score)
    peak = jnp.max(scores, -1, keepdims=True)
    weights = jnp.exp(scores - peak)
    return weights / jnp.sum(weights, -1, keepdims=True)


def heads_of(rows):
    return rows.reshape(2, -1, HEADS, HEAD_DIM)


def local_forward(queries, keys_values, visible):
    width = queries.shape[1]
    keys, values = keys_values[..., :width], keys_values[..., width:]
    probs = local_scores(heads_of(queries), heads_of(keys), visible)
    attended = jnp.einsum(
        "bhqk,bkhd->bqhd", probs.astype(BF), heads_of(values), preferred_element_type=F32
    )
    return attended.reshape(queries.shape).astype(BF), probs


def local_backward(d_attended, probs, queries, keys_values, count):
    rows, width = queries.shape
    row_count = rows // 2
    keys, values = keys_values[..., :width], keys_values[..., width:]
    d_heads = heads_of(d_attended)
    d_probs = jnp.einsum(
        "bqhd,bkhd->bhqk", d_heads, heads_of(values), preferred_element_type=F32
    )
    delta = jnp.sum(probs * d_probs, -1, keepdims=True)
    d_scores = (probs * (d_probs - delta)).astype(BF)
    d_queries = (
        jnp.einsum("bhqk,bkhd->bqhd", d_scores, heads_of(keys), preferred_element_type=F32) * SCALE
    )
    d_keys = (
        jnp.einsum("bhqk,bqhd->bkhd", d_scores, heads_of(queries), preferred_element_type=F32)
        * SCALE
    )
    d_values = jnp.einsum(
        "bhqk,bqhd->bkhd", probs.astype(BF), d_heads, preferred_element_type=F32
    )
    d_kv = jnp.concatenate(
        [d_keys.reshape(2, -1, width), d_values.reshape(2, -1, width)], 2
    )
    to_before = d_kv[:, :row_count].astype(BF)
    to_after = d_kv[:, 2 * row_count :].astype(BF)
    from_after = lax.ppermute(to_before, "dp", neighbours(count, -1))
    from_before = lax.ppermute(to_after, "dp", neighbours(count, 1))
    d_kv = d_kv[:, row_count : 2 * row_count] + from_after.astype(F32) + from_before.astype(F32)
    d_kv = d_kv.reshape(rows, 2 * width)
    return d_queries.reshape(rows, width), d_kv[:, :width], d_kv[:, width:]


def split_heads(rows):
    row_count = rows.shape[0] // 2
    half = row_count // 2
    parts = rows.reshape(2, row_count, 4, 3, HEAD_DIM)
    own = parts[:, :, :, 0::2].transpose(0, 2, 3, 1, 4)
    shared = parts[:, :, :, 1].reshape(2, 2, half, 4, HEAD_DIM).transpose(0, 3, 1, 2, 4)
    return jnp.concatenate([own, shared], 3).reshape(GROUP, row_count + half, HEAD_DIM)


def join_heads(blocks):
    row_count = blocks.shape[1] * 2 // 3
    half = row_count // 2
    parts = blocks.reshape(2, 4, 2, row_count + half, HEAD_DIM)
    own = parts[:, :, :, :row_count].transpose(0, 3, 1, 2, 4)
    shared = parts[:, :, :, row_count:].transpose(0, 2, 3, 1, 4).reshape(2, row_count, 4, HEAD_DIM)
    rows = jnp.stack([own[:, :, :, 0], shared, own[:, :, :, 1]], 3)
    return rows.reshape(2 * row_count, HEADS * HEAD_DIM)


def fold(blocks):
    half = blocks.shape[1] // 2
    return jnp.concatenate([blocks[:, :half], blocks[:, half:]], 2)


def unfold(blocks):
    return jnp.concatenate([blocks[..., :HEAD_DIM], blocks[..., HEAD_DIM:]], 1)


def exchange(blocks, count):
    groups = [list(range(s, s + GROUP)) for s in range(0, count, GROUP)]
    return lax.all_to_all(blocks, "dp", 0, 0, axis_index_groups=groups)


def other_core(rows, count):
    return lax.ppermute(rows, "dp", [(i, i ^ 1) for i in range(count)])


def pack_three(first, second, third):
    return jnp.concatenate([jnp.concatenate([first, second], 2), fold(third)], 1)


def unpack_three(blocks):
    rows = blocks.shape[1] * 2 // 3
    pair = blocks[:, :rows]
    return pair[..., :HEAD_DIM], pair[..., HEAD_DIM:], unfold(blocks[:, rows:])


def own_rows(blocks):
    row_count = blocks.shape[1] * 2 // 3
    return blocks[:, :row_count].reshape(-1, HEAD_DIM)


def shared_rows(blocks):
    row_count = blocks.shape[1] * 2 // 3
    return blocks[:, row_count:].reshape(-1, HEAD_DIM)


def to_blocks(own, shared):
    return jnp.concatenate(
        [own.reshape(GROUP, -1, HEAD_DIM), shared.reshape(GROUP, -1, HEAD_DIM)], 1
    )


def soft_attend(queries, keys, values, query_seg, key_seg):
    raw = dot_bt(queries, keys) * SCALE
    scores = jnp.where(query_seg[:, None] == key_seg[None, :], raw, masked_score)
    peak = jnp.max(scores, -1, keepdims=True)
    weights = jnp.exp(scores - peak)
    probs = weights / jnp.sum(weights, -1, keepdims=True)
    return dot(probs.astype(BF), values), probs


def soft_back(d_out, probs, queries, keys, values):
    d_probs = dot_bt(d_out, values)
    delta = jnp.sum(probs * d_probs, -1, keepdims=True)
    d_scores = (probs * (d_probs - delta)).astype(BF)
    d_queries = dot(d_scores, keys) * SCALE
    d_keys = dot_at(d_scores, queries) * SCALE
    d_values = dot_at(probs.astype(BF), d_out)
    return d_queries, d_keys, d_values


def global_forward(queries, keys, values, own_seg, shared_seg, count):
    sent = pack_three(split_heads(queries), split_heads(keys), split_heads(values))
    got_q, got_k, got_v = unpack_three(exchange(sent, count))
    shared_kv = jnp.concatenate([shared_rows(got_k), shared_rows(got_v)], 1)
    both_kv = jnp.concatenate([shared_kv, other_core(shared_kv, count)], 0)
    own_in = (own_rows(got_q), own_rows(got_k), own_rows(got_v))
    shared_in = (shared_rows(got_q), both_kv[:, :HEAD_DIM], both_kv[:, HEAD_DIM:])
    own_out, own_probs = soft_attend(*own_in, own_seg, own_seg)
    shared_out, shared_probs = soft_attend(
        *shared_in, shared_seg[: shared_seg.shape[0] // 2], shared_seg
    )
    back = fold(to_blocks(own_out.astype(BF), shared_out.astype(BF)))
    attended = join_heads(unfold(exchange(back, count)))
    return attended, (own_in, own_probs, shared_in, shared_probs)


def global_backward(d_attended, saved, count):
    own_in, own_probs, shared_in, shared_probs = saved
    got = unfold(exchange(fold(split_heads(d_attended)), count))
    own_grads = soft_back(own_rows(got), own_probs, *own_in)
    shared_q, shared_k, shared_v = soft_back(shared_rows(got), shared_probs, *shared_in)
    d_kv = jnp.concatenate([shared_k, shared_v], 1)
    half = d_kv.shape[0] // 2
    d_kv = d_kv[:half] + other_core(d_kv[half:].astype(BF), count).astype(F32)
    shared_grads = (shared_q, d_kv[:, :HEAD_DIM], d_kv[:, HEAD_DIM:])
    blocks = [
        to_blocks(own.astype(BF), shared.astype(BF))
        for own, shared in zip(own_grads, shared_grads)
    ]
    back = unpack_three(exchange(pack_three(*blocks), count))
    return tuple(join_heads(part).astype(F32) for part in back)


def to_other_section(rows, step):
    return lax.ppermute(rows, "section", [(0, 1)] if step > 0 else [(1, 0)])


def on_device(
    tokens_in,
    segment_ids,
    out_grad,
    qkv_weight,
    attn_out_weight,
    mlp_in_weight,
    mlp_out_weight,
    attn_gain,
    mlp_gain,
):
    lower = lax.axis_index("section") == 0
    count = lax.axis_size("dp")
    replica = lax.axis_index("dp")
    group_pos = replica % GROUP
    micro_count, row_count, width = tokens_in.shape
    shard = qkv_weight.shape[1]
    wide = mlp_out_weight.shape[1] * width // shard
    gains = jnp.stack([attn_gain[0], mlp_gain[0]], 1)
    gains = jnp.pad(gains, ((0, 0), (0, 126)))
    first = lax.all_gather(
        jnp.concatenate([qkv_weight[0], gains], 1), "dp", axis=0, tiled=True
    )
    second = lax.all_gather(
        jnp.concatenate(
            [attn_out_weight[0], mlp_in_weight[0], mlp_out_weight[0].reshape(shard, wide)], 1
        ),
        "dp",
        axis=0,
        tiled=True,
    )
    weights = {
        "qkv": first[:, : 3 * width],
        "gain_attn": first[:, 3 * width].astype(F32)[None],
        "gain_mlp": first[:, 3 * width + 1].astype(F32)[None],
        "attn": second[:, :width],
        "mlp_in": second[:, width : second.shape[1] - wide],
        "mlp_out": second[:, second.shape[1] - wide :].reshape(-1, width),
    }

    groups = [list(range(s, s + GROUP)) for s in range(0, count, GROUP)]
    segments = lax.all_gather(segment_ids, "dp", axis=1, tiled=True, axis_index_groups=groups)
    positions = group_pos * row_count + jnp.arange(row_count)
    local_tables = angles(positions, local_log_base)
    global_tables = angles(positions, global_log_base)

    key_pos = positions[0] - row_count + jnp.arange(3 * row_count)
    around = jnp.pad(segments, ((0, 0), (row_count, row_count)), constant_values=-1)
    key_seg = lax.dynamic_slice_in_dim(around, group_pos * row_count, 3 * row_count, 1)
    visible = (segment_ids[:, :, None] == key_seg[:, None, :]) & (
        jnp.abs(positions[:, None] - key_pos[None, :]) <= HALF_WIN
    )[None]

    own_seg = lax.dynamic_index_in_dim(segments, group_pos // 8, 0, keepdims=False)
    halves = own_seg.reshape(GROUP, 2, row_count // 2)
    mine = lax.dynamic_index_in_dim(halves, group_pos % 2, 1, keepdims=False).reshape(-1)
    theirs = lax.dynamic_index_in_dim(halves, 1 - group_pos % 2, 1, keepdims=False).reshape(-1)
    shared_seg = jnp.concatenate([mine, theirs])

    in_0 = tokens_in.reshape(-1, width).astype(F32)
    normed_0, q_0, k_0, v_0 = project(in_0, weights, local_tables)
    kv_0 = with_halo(jnp.concatenate([k_0, v_0], 1).reshape(2, row_count, 2 * width), count)
    att_0, probs_0 = local_forward(q_0, kv_0, visible)
    out_0, saved_0 = finish_forward(in_0, att_0, weights)

    in_1 = to_other_section(out_0, 1).astype(F32)
    normed_1, q_1, k_1, v_1 = project(in_1, weights, global_tables)
    att_1, kept_1 = global_forward(q_1, k_1, v_1, own_seg, shared_seg, count)
    out_1, saved_1 = finish_forward(in_1, att_1, weights)

    up_1 = out_grad.reshape(-1, width).astype(F32)
    d_mid_1, d_att_1, ops_1, gain_mlp_1 = start_backward(up_1, saved_1, weights)
    d_q, d_k, d_v = global_backward(d_att_1, kept_1, count)
    d_proj_1 = jnp.concatenate(
        [unrotate(d_q, global_tables), unrotate(d_k, global_tables), d_v], 1
    ).astype(BF)
    grad_1, gain_attn_1 = finish_backward(d_mid_1, d_proj_1, in_1, weights)

    up_0 = to_other_section(grad_1, -1).astype(F32)
    d_mid_0, d_att_0, ops_0, gain_mlp_0 = start_backward(up_0, saved_0, weights)
    n2, d_gu, mixed, d_mlp, d_attn = (
        jnp.where(lower, a, b) for a, b in zip(ops_0, ops_1)
    )
    mlp_grads = jnp.concatenate(
        [
            dot_at(n2, d_gu).astype(BF),
            dot_at(mixed, d_mlp).astype(BF).reshape(width, -1),
        ],
        1,
    )
    mlp_share = lax.psum_scatter(mlp_grads, "dp", scatter_dimension=0, tiled=True)
    d_q, d_k, d_v = local_backward(d_att_0, probs_0, q_0, kv_0, count)
    d_proj_0 = jnp.concatenate(
        [unrotate(d_q, local_tables), unrotate(d_k, local_tables), d_v], 1
    ).astype(BF)
    grad_0, gain_attn_0 = finish_backward(d_mid_0, d_proj_0, in_0, weights)

    n1, d_proj, att = (
        jnp.where(lower, a, b)
        for a, b in ((normed_0, normed_1), (d_proj_0, d_proj_1), (att_0, att_1))
    )
    gain_grads = jnp.where(
        lower,
        jnp.stack([gain_attn_0, gain_mlp_0], 1),
        jnp.stack([gain_attn_1, gain_mlp_1], 1),
    )
    attn_grads = jnp.concatenate(
        [
            dot_at(n1, d_proj).astype(BF),
            dot_at(att, d_attn).astype(BF),
            jnp.pad(gain_grads, ((0, 0), (0, 126))).astype(BF),
        ],
        1,
    )
    attn_share = lax.psum_scatter(attn_grads, "dp", scatter_dimension=0, tiled=True)
    mlp_share, attn_share = mlp_share.astype(F32), attn_share.astype(F32)
    return (
        jnp.where(lower, out_0, out_1).reshape(1, micro_count, row_count, width),
        jnp.where(lower, grad_0, grad_1).reshape(1, micro_count, row_count, width),
        attn_share[None, :, : 3 * width],
        attn_share[None, :, 3 * width : 4 * width],
        mlp_share[None, :, : mlp_share.shape[1] - wide],
        mlp_share[:, mlp_share.shape[1] - wide :].reshape(1, -1, width),
        attn_share[None, :, 4 * width],
        attn_share[None, :, 4 * width + 1],
    )


def solution(mesh):
    in_specs = (
        P(None, "dp", None),
        P(None, "dp"),
        P(None, "dp", None),
        P("section", "dp", None),
        P("section", "dp", None),
        P("section", "dp", None),
        P("section", "dp", None),
        P("section", "dp"),
        P("section", "dp"),
    )
    out_specs = (
        P("section", None, "dp", None),
        P("section", None, "dp", None),
        P("section", "dp", None),
        P("section", "dp", None),
        P("section", "dp", None),
        P("section", "dp", None),
        P("section", "dp"),
        P("section", "dp"),
    )
    return jax.shard_map(
        on_device, mesh=mesh, in_specs=in_specs, out_specs=out_specs, check_vma=False
    )
```

time: 1270 us -> 597 us (0.47)
  waiting for transfers between devices: 697 us -> 234 us
  other arithmetic: 142 us -> 55.2 us
  matrix products: 129 us -> 71.8 us
  local copies, waits for them, and re-layouts: 156 us -> 120 us
  starting transfers between devices: 48.2 us -> 19 us
    ppermute x44 -> x8, waiting for transfers between devices: 514 us -> 7.99 us  [the longest x2 7.97 us: to_other_section(): return lax.ppermute(rows, 'section', [(0, 1)] if step > 0 else [(1, 0)])]
    select_n x57 -> x1, other arithmetic: 75.3 us -> 0.91 us  [on_device(): jnp.where(lower, grad_0, grad_1).reshape(1, micro_count, row_count, width)]
    unnamed x2 -> x0, blocking collectives: 66.7 us -> none
    dot_general x52 -> x37, matrix products: 129 us -> 71 us  [the longest x12 24.5 us: dot_bt(): lax.dot_general(left, right, (((1,), (1,)), ((), ())), preferred_element_...]
    slice x36 -> x50, local copies, waits for them, and re-layouts: 72.2 us -> 21.9 us  [the longest x6 5.93 us: fold(): return jnp.concatenate([blocks[:, :half], blocks[:, half:]], 2)]
    all_to_all x0 -> x3, blocking collectives: none -> 45.7 us  [exchange(): return lax.all_to_all(blocks, 'dp', 0, 0, axis_index_groups=groups)]
    ppermute x44 -> x8, starting transfers between devices: 47.6 us -> 14.7 us  [the longest x2 5.13 us: to_other_section(): return lax.ppermute(rows, 'section', [(0, 1)] if step > 0 else [(1, 0)])]
    all_gather x0 -> x1, blocking collectives: none -> 25.6 us  [on_device(): lax.all_gather(segment_ids, 'dp', axis=1, tiled=True, axis_index_groups=g...]
  transfers between devices with their start and end apart: 52 -> 13, of which waited for: 39 -> 7; matrix products, arithmetic and copies ran while one was open for 19% -> 10% of each run, Pallas kernels for 0% -> 0%
where the time goes in v1:
time: 597 us; the launch traced here: 588 us
  waiting for transfers between devices  234 us (39%)
  local copies, waits for them, and re-layouts  120 us (20%)
  matrix products  71.8 us (12%)
  blocking collectives  71.3 us (12%)
  other arithmetic  55.2 us (9%)
  starting transfers between devices  19 us (3%)
  between operations  16.7 us (3%)
    reduce_scatter x1, waiting for transfers between devices, on_device(): lax.psum_scatter(mlp_grads, 'dp', scatter_dimension=0, tiled=True)  79.6 us
    reduce_scatter x1, waiting for transfers between devices, on_device(): lax.psum_scatter(attn_grads, 'dp', scatter_dimension=0, tiled=True)  58.6 us
    all_gather x1, waiting for transfers between devices, on_device(): lax.all_gather(jnp.concatenate([qkv_weight[0], gains], 1), 'dp', axis=0,...  47 us
    all_to_all x3, blocking collectives, exchange(): return lax.all_to_all(blocks, 'dp', 0, 0, axis_index_groups=groups)  45.7 us
    all_gather x1, waiting for transfers between devices, on_device(): lax.all_gather(jnp.concatenate([attn_out_weight[0], mlp_in_weight[0], mlp...  27.3 us
    all_gather x1, blocking collectives, on_device(): lax.all_gather(segment_ids, 'dp', axis=1, tiled=True, axis_index_groups=g...  25.6 us
    dot_general x12, matrix products, dot_bt(): lax.dot_general(left, right, (((1,), (1,)), ((), ())), preferred_element_...  24.5 us
    dot_general x12, matrix products, dot(): return jnp.dot(left, right, preferred_element_type=F32)  20.1 us
  transfers between devices with their start and end apart: 13, of which 7 were waited for; matrix products, arithmetic and copies ran while one was open for 10% of the time, Pallas kernels for 0%

profile of v1, /device:TPU:0, one launch (start us, length us, event | category | flops | bytes accessed | tf_op | source)
XLA Modules:
  0.0 587.7 jit_solution(15304291027087225531)
XLA Ops:
  14.4 47.0 %all-gather.4.cloned.1.call-done = bf16[768,2432]{1,0:T(8,128)(2,1)} async-done(((bf16[48,2432]{1,0:T(8,128)(2,1)}), bf16[768,2432]{1,0:T(8,128)(2,1)}) %all-gather.4.cloned.1.call-update) | async-done | bytes 3735568 | tf_op jit(solution)/shard_map/all_gather | solution.py:330
  62.8 2.7 fusion.21
  68.0 3.1 collective-permute-start
  71.2 25.6 %all-gather = s32[16,64,2]{1,2,0:T(2,128)S(1)} all-gather(s32[1,64,2]{1,2,0:T(2,128)S(1)} %bitcast.290), channel_id=1, replica_groups={{0,1,2,3,4,5,6,7,8,9,10,11,12,13,14,15},{16,17,18,19,20,21,22,23,24,25,..., dimensions={0}, use_global_device_ids=true | all-gather | bytes 8704 | tf_op jit(solution)/shard_map/all_gather | solution.py:351
  100.3 2.1 fusion.28
  103.1 27.3 %all-gather.6.cloned.1.call-done = bf16[768,4224]{1,0:T(8,128)(2,1)} async-done(((bf16[48,4224]{1,0:T(8,128)(2,1)}), bf16[768,4224]{1,0:T(8,128)(2,1)}) %all-gather.6.cloned.1.call-update) | async-done | bytes 6488080 | tf_op jit(solution)/shard_map/all_gather | solution.py:333
  132.3 2.7 fusion.13
  139.0 2.4 reshape.547
  143.3 3.6 collective-permute-start.2
  147.5 3.8 collective-permute-done.2
  152.4 2.7 fusion.19
  167.4 3.6 all-to-all-start
  172.8 13.6 %all-to-all-done = bf16[16,144,128]{2,1,0:T(8,128)(2,1)S(1)} async-done(((bf16[16,144,128]{2,1,0:T(8,128)(2,1)}), bf16[16,144,128]{2,1,0:T(8,128)(2,1)S(1)}, u32[]{:S(2)}, u32[]{:S(2)}) %all-to-all-start) | async-done | bytes 589856 | tf_op jit(solution)/shard_map/all_to_all | solution.py:221
  198.7 13.9 %all_to_all.20 = bf16[16,48,128]{2,1,0:T(8,128)(2,1)S(1)} all-to-all(bf16[16,48,128]{2,1,0:T(8,128)(2,1)S(1)} %fusion.123), channel_id=1, replica_groups={{0,1,2,3,4,5,6,7,8,9,10,11,12,13,14,15},{16,17,18,19,20,21,22,23,24,25,..., dimensions={0} | all-to-all | bytes 393216 | tf_op jit(solution)/shard_map/all_to_all | solution.py:221
  219.9 2.8 fusion.11
  222.8 2.6 fusion.60
  246.6 11.7 %all_to_all.21 = bf16[16,48,128]{2,1,0:T(8,128)(2,1)S(1)} all-to-all(bf16[16,48,128]{2,1,0:T(8,128)(2,1)S(1)} %pad_maximum_fusion.34), channel_id=1, replica_groups={{0,1,2,3,4,5,6,7,8,9,10,11,12,13,14,15},{16,17,18,19,20,21,22,23,24,25,..., dimensions={0} | all-to-all | bytes 393216 | tf_op jit(solution)/shard_map/all_to_all | solution.py:221
  258.6 3.8 convolution_convert_fusion.8
  270.1 2.5 multiply_reduce_fusion.1
  276.5 2.8 multiply_convert_fusion.1
  283.2 20.1 %all_to_all.22 = bf16[16,144,128]{2,1,0:T(8,128)(2,1)S(1)} all-to-all(bf16[16,144,128]{2,1,0:T(8,128)(2,1)S(1)} %fusion.69), channel_id=1, replica_groups={{0,1,2,3,4,5,6,7,8,9,10,11,12,13,14,15},{16,17,18,19,20,21,22,23,24,25,..., dimensions={0} | all-to-all | bytes 1179648 | tf_op jit(solution)/shard_map/all_to_all | solution.py:221
  317.6 2.2 copy.434
  319.8 2.1 reshape.605
  325.0 2.3 reshape.597
  334.8 3.7 fusion.104
  344.4 4.2 collective-permute-done.5
  348.6 2.2 fusion.66
  350.9 3.6 multiply_reduce_fusion.4
  358.1 2.1 copy.413
  360.3 3.5 multiply_reduce_fusion.2
  365.4 2.9 copy.415
  368.3 2.4 multiply_convert_fusion.2
  373.1 2.9 copy.414
  380.1 3.8 collective-permute-start.7
  386.7 2.6 copy.435
  389.2 2.4 reshape_reshape.6
  391.6 2.2 reshape.606
  393.9 2.7 convolution_convert_fusion.3
  399.7 1.9 broadcast_multiply_fusion.3
  408.0 4.3 multiply_reduce_fusion.5
  414.2 2.6 convolution_convert_fusion.1
  416.8 2.6 fusion.2
  420.5 2.8 convolution_convert_fusion.2
  423.3 4.1 reshape.589
  427.4 2.6 convolution_convert_fusion
  430.0 2.7 pad_maximum_fusion
  435.8 58.6 %reduce-scatter.3.cloned.1.call-done = bf16[48,3200]{1,0:T(8,128)(2,1)} async-done(((bf16[768,3200]{1,0:T(8,128)(2,1)}), bf16[48,3200]{1,0:T(8,128)(2,1)}) %reduce-scatter.3.cloned.1.call-update) | async-done | bytes 307216 | tf_op jit(solution)/shard_map/reduce_scatter | solution.py:424
  497.5 79.6 %reduce-scatter.5.cloned.1.call-done = bf16[48,3456]{1,0:T(8,128)(2,1)} async-done(((bf16[768,3456]{1,0:T(8,128)(2,1)}), bf16[48,3456]{1,0:T(8,128)(2,1)}) %reduce-scatter.5.cloned.1.call-update) | async-done | bytes 331792 | tf_op jit(solution)/shard_map/reduce_scatter | solution.py:400
  (505 shorter events, 161.0 us)
Async XLA Ops:
  7.2 5.4 copy-start.15
  7.2 54.2 %all-gather.4.cloned.1.call-start = ((), (), s32[]{:S(2)}) async-start(), calls=%async_computation.6 | async-start | bytes 3969024 | tf_op jit(solution)/shard_map/all_gather | solution.py:330
  9.7 120.6 %all-gather.6.cloned.1.call-start = ((), (), s32[]{:S(2)}) async-start(), calls=%async_computation.7 | async-start | bytes 6893568 | tf_op jit(solution)/shard_map/all_gather | solution.py:333
  12.8 52.8 %copy-start.97 = (f32[128]{0:T(128)}, f32[128]{0:T(128)S(1)}, u32[]{:S(2)}) copy-start(f32[128]{0:T(128)S(1)} %div.93) | copy-start | bytes 1540
  13.1 52.5 %copy-start.99 = (f32[128]{0:T(128)}, f32[128]{0:T(128)S(1)}, u32[]{:S(2)}) copy-start(f32[128]{0:T(128)S(1)} %rsqrt.38) | copy-start | bytes 1540
  14.3 52.2 %copy-start.23 = (f32[128,768]{1,0:T(8,128)}, f32[128,768]{1,0:T(8,128)S(1)}, u32[]{:S(2)}) copy-start(f32[128,768]{1,0:T(8,128)S(1)} %copy.326) | copy-start | bytes 1179652
  66.3 4.8 copy-start.96
  66.7 31.1 %collective-permute-start.1 = (bf16[2,64,1536]{2,1,0:T(8,128)(2,1)S(1)}, bf16[2,64,1536]{2,1,0:T(8,128)(2,1)S(1)}, u32[]{:S(2)}, u32[]{:S(2)}) collective-permute-start(bf16[2,64,1536]{2,1,0:T(8,128)(2,1)S(1)} %bitcast.225), channel_id=1, source_target_pairs={{1,0},{2,1},{3,2},{4,3},{5,4},{6,5},{7,6},{8,7},{9,8},{10,9},{11,1... | collective-permute-start | bytes 1179656 | tf_op jit(solution)/shard_map/ppermute | solution.py:133
  68.0 29.8 %collective-permute-start = (bf16[2,64,1536]{2,1,0:T(8,128)(2,1)S(1)}, bf16[2,64,1536]{2,1,0:T(8,128)(2,1)S(1)}, u32[]{:S(2)}, u32[]{:S(2)}) collective-permute-start(bf16[2,64,1536]{2,1,0:T(8,128)(2,1)S(1)} %bitcast.226), channel_id=1, source_target_pairs={{0,1},{1,2},{2,3},{3,4},{4,5},{5,6},{6,7},{7,8},{8,9},{9,10},{10,1... | collective-permute-start | bytes 1179656 | tf_op jit(solution)/shard_map/ppermute | solution.py:132
  103.1 31.9 %copy-start.36 = (bf16[128,768]{0,1:T(8,128)(2,1)}, bf16[128,768]{0,1:T(8,128)(2,1)S(1)}, u32[]{:S(2)}) copy-start(bf16[128,768]{0,1:T(8,128)(2,1)S(1)} %convert_element_type.250) | copy-start | bytes 589828
  141.3 5.6 copy-start.73
  143.3 8.3 %copy-start.62 = (bf16[128,768]{1,0:T(8,128)(2,1)}, bf16[128,768]{1,0:T(8,128)(2,1)S(1)}, u32[]{:S(2)}) copy-start(bf16[128,768]{1,0:T(8,128)(2,1)S(1)} %fusion.32) | copy-start | bytes 589828
  143.3 8.0 %collective-permute-start.2 = (bf16[128,768]{1,0:T(8,128)(2,1)S(1)}, bf16[128,768]{1,0:T(8,128)(2,1)S(1)}, u32[]{:S(2)}, u32[]{:S(2)}) collective-permute-start(bf16[128,768]{1,0:T(8,128)(2,1)S(1)} %fusion.32), channel_id=1, source_target_pairs={{0,16},{1,17},{2,18},{3,19},{4,20},{5,21},{6,22},{7,23},{8,24},{9,... | collective-permute-start | bytes 589832 | tf_op jit(solution)/shard_map/ppermute | solution.py:307
  147.5 13.3 %copy-start.24 = (f32[128,768]{1,0:T(8,128)}, f32[128,768]{1,0:T(8,128)S(1)}, u32[]{:S(2)}) copy-start(f32[128,768]{1,0:T(8,128)S(1)} %copy.338) | copy-start | bytes 1179652
  165.7 6.2 %copy-start.75 = (s32[1024,2]{0,1:T(2,128)S(1)}, s32[1024,2]{0,1:T(2,128)}, u32[]{:S(2)}) copy-start(s32[1024,2]{0,1:T(2,128)} %copy-done.74) | copy-start | bytes 24580
  167.4 19.1 %all-to-all-start = ((bf16[16,144,128]{2,1,0:T(8,128)(2,1)}), bf16[16,144,128]{2,1,0:T(8,128)(2,1)S(1)}, u32[]{:S(2)}, u32[]{:S(2)}) async-start(bf16[16,144,128]{2,1,0:T(8,128)(2,1)} %copy.356), calls=%async_computation | async-start | bytes 1179648 | tf_op jit(solution)/shard_map/all_to_all | solution.py:221
  171.0 323.3 %reduce-scatter.3.cloned.1.call-start = ((), (), s32[]{:S(2)}) async-start(), calls=%async_computation.8 | async-start | bytes 5222400 | tf_op jit(solution)/shard_map/reduce_scatter | solution.py:424
  186.6 8.7 %copy-start.64 = (bf16[16,32,64]{2,1,0:T(8,128)(2,1)}, bf16[16,32,64]{2,1,0:T(8,128)(2,1)S(1)}, u32[]{:S(2)}) copy-start(bf16[16,32,64]{2,1,0:T(8,128)(2,1)S(1)} %get-tuple-element.55) | copy-start | bytes 196612
  186.8 8.4 %collective-permute-start.3 = (bf16[512,128]{1,0:T(8,128)(2,1)S(1)}, bf16[512,128]{1,0:T(8,128)(2,1)S(1)}, u32[]{:S(2)}, u32[]{:S(2)}) collective-permute-start(bf16[512,128]{1,0:T(8,128)(2,1)S(1)} %pad_maximum_fusion.35), channel_id=1, source_target_pairs={{0,1},{1,0},{2,3},{3,2},{4,5},{5,4},{6,7},{7,6},{8,9},{9,8},{10,11... | collective-permute-start | bytes 393224 | tf_op jit(solution)/shard_map/ppermute | solution.py:225
  217.8 4.9 copy-start.38
  217.8 4.9 copy-start.61
  219.6 7.7 %copy-start.86 = (f32[128]{0:T(128)}, f32[128]{0:T(128)S(1)}, u32[]{:S(2)}) copy-start(f32[128]{0:T(128)S(1)} %broadcast_multiply_fusion.15) | copy-start | bytes 1540
  219.9 7.5 %copy-start.92 = (f32[128]{0:T(128)}, f32[128]{0:T(128)S(1)}, u32[]{:S(2)}) copy-start(f32[128]{0:T(128)S(1)} %add_rsqrt_fusion.1) | copy-start | bytes 1540
  219.9 5.5 slice-start
  270.1 6.5 %copy-start.79 = (f32[512]{0:T(512)S(1)}, f32[512]{0:T(512)}, u32[]{:S(2)}) copy-start(f32[512]{0:T(512)} %copy-done.78) | copy-start | bytes 6148
  270.1 6.5 %copy-start.81 = (f32[512]{0:T(512)S(1)}, f32[512]{0:T(512)}, u32[]{:S(2)}) copy-start(f32[512]{0:T(512)} %copy-done.80) | copy-start | bytes 6148
  279.8 1.8 collective-permute-start.4
  312.3 9.6 %copy-start.26 = (f32[2,64,4,3,64]{1,0,4,3,2:T(2,128)S(1)}, f32[2,64,4,3,64]{1,0,4,3,2:T(2,128)}, u32[]{:S(2)}) copy-start(f32[2,64,4,3,64]{1,0,4,3,2:T(2,128)} %copy.386) | copy-start | bytes 1179652
  330.2 4.4 copy-start.25
  334.8 6.2 %copy-start.37 = (bf16[128,768]{0,1:T(8,128)(2,1)S(1)}, bf16[128,768]{0,1:T(8,128)(2,1)}, u32[]{:S(2)}) copy-start(bf16[128,768]{0,1:T(8,128)(2,1)} %copy-done.36) | copy-start | bytes 589828
  334.8 8.7 %copy-start.101 = (bf16[768]{0:T(1024)(128)(2,1)S(1)}, bf16[768]{0:T(1024)(128)(2,1)}, u32[]{:S(2)}) copy-start(bf16[768]{0:T(1024)(128)(2,1)} %get-tuple-element.10) | copy-start | bytes 4612
  338.5 10.1 %copy-start.6 = (bf16[1152,768]{1,0:T(8,128)(2,1)S(1)}, bf16[1152,768]{1,0:T(8,128)(2,1)}, u32[]{:S(2)}) copy-start(bf16[1152,768]{1,0:T(8,128)(2,1)} %reshape.547) | copy-start | bytes 5308420
  339.4 9.2 %collective-permute-start.5 = (bf16[128,768]{1,0:T(8,128)(2,1)}, bf16[128,768]{1,0:T(8,128)(2,1)}, u32[]{:S(2)}, u32[]{:S(2)}) collective-permute-start(bf16[128,768]{1,0:T(8,128)(2,1)} %fusion.103), channel_id=1, source_target_pairs={{16,0},{17,1},{18,2},{19,3},{20,4},{21,5},{22,6},{23,7},{24,8},{25... | collective-permute-start | bytes 589832 | tf_op jit(solution)/shard_map/ppermute | solution.py:307
  343.5 7.3 %copy-start.85 = (f32[128]{0:T(128)S(1)}, f32[128]{0:T(128)}, u32[]{:S(2)}) copy-start(f32[128]{0:T(128)} %copy-done.84) | copy-start | bytes 1540
  343.5 7.3 %copy-start.89 = (f32[128]{0:T(128)S(1)}, f32[128]{0:T(128)}, u32[]{:S(2)}) copy-start(f32[128]{0:T(128)} %copy-done.88) | copy-start | bytes 1540
  348.6 7.8 %slice-start.2 = ((s8[6488064]{0:T(1024)(128)(4,1)}), s8[4194304]{0:T(1024)(128)(4,1)S(1)}, s32[]{:S(2)}) async-start(s8[6488064]{0:T(1024)(128)(4,1)} %bitcast.198), calls=%async_computation.12 | async-start | bytes 8388608
  350.9 5.6 slice-start.3
  354.6 5.7 copy-start.83
  376.0 7.9 %copy-start.12 = (bf16[2,12,64,192]{3,2,1,0:T(8,128)(2,1)S(1)}, bf16[2,12,64,192]{3,2,1,0:T(8,128)(2,1)}, u32[]{:S(2)}) copy-start(bf16[2,12,64,192]{3,2,1,0:T(8,128)(2,1)} %copy-done.11) | copy-start | bytes 1769476
  376.0 7.9 %copy-start.28 = (bf16[2,192,768]{1,2,0:T(8,128)(2,1)S(1)}, bf16[2,192,768]{1,2,0:T(8,128)(2,1)}, u32[]{:S(2)}) copy-start(bf16[2,192,768]{1,2,0:T(8,128)(2,1)} %copy-done.27) | copy-start | bytes 1769476
  378.8 17.7 %collective-permute-start.6 = (bf16[2,64,1536]{2,1,0:T(8,128)(2,1)}, bf16[2,64,1536]{2,1,0:T(8,128)(2,1)}, u32[]{:S(2)}, u32[]{:S(2)}) collective-permute-start(bf16[2,64,1536]{2,1,0:T(8,128)(2,1)} %get-tuple-element.36), channel_id=1, source_target_pairs={{1,0},{2,1},{3,2},{4,3},{5,4},{6,5},{7,6},{8,7},{9,8},{10,9},{11,1... | collective-permute-start | bytes 1179656 | tf_op jit(solution)/shard_map/ppermute | solution.py:184
  380.1 16.5 %collective-permute-start.7 = (bf16[2,64,1536]{2,1,0:T(8,128)(2,1)}, bf16[2,64,1536]{2,1,0:T(8,128)(2,1)}, u32[]{:S(2)}, u32[]{:S(2)}) collective-permute-start(bf16[2,64,1536]{2,1,0:T(8,128)(2,1)} %get-tuple-element.37), channel_id=1, source_target_pairs={{0,1},{1,2},{2,3},{3,4},{4,5},{5,6},{6,7},{7,8},{8,9},{9,10},{10,1... | collective-permute-start | bytes 1179656 | tf_op jit(solution)/shard_map/ppermute | solution.py:185
  386.6 7.2 %copy-start.59 = (bf16[128,768]{1,0:T(8,128)(2,1)S(1)}, bf16[128,768]{1,0:T(8,128)(2,1)}, u32[]{:S(2)}) copy-start(bf16[128,768]{1,0:T(8,128)(2,1)} %copy.419) | copy-start | bytes 589828
  408.0 4.4 copy-start.57
  408.0 4.4 copy-start.58
  408.0 6.2 %copy-start.35 = (bf16[128,768]{1,0:T(8,128)(2,1)S(1)}, bf16[128,768]{1,0:T(8,128)(2,1)}, u32[]{:S(2)}) copy-start(bf16[128,768]{1,0:T(8,128)(2,1)} %copy-done.34) | copy-start | bytes 589828
  408.0 6.2 %copy-start.55 = (bf16[128,768]{1,0:T(8,128)(2,1)S(1)}, bf16[128,768]{1,0:T(8,128)(2,1)}, u32[]{:S(2)}) copy-start(bf16[128,768]{1,0:T(8,128)(2,1)} %copy-done.54) | copy-start | bytes 589828
  419.4 157.7 %reduce-scatter.5.cloned.1.call-start = ((), (), s32[]{:S(2)}) async-start(), calls=%async_computation.9 | async-start | bytes 5640192 | tf_op jit(solution)/shard_map/reduce_scatter | solution.py:400
  (73 other events, 166.6 us)
Sparse Core Ops, SparseCore 0:
  10.8 50.5 all-gather.3
  64.1 66.1 all-gather.5
  419.6 74.7 reduce-scatter.2
  498.8 78.3 reduce-scatter.4
